TPU v7x, 256 devices: a whole 4x4x8 slice. The times are simulated.
256 devices in a mesh: particle: 16 (over x, y_lo, core), shard: 16 (over z, y_hi).
Axes of the slice: x: 4, y: 4 (y_hi: 2, y_lo: 2; y = y_hi * 2 + y_lo), z: 8, core: 2. Of those that a mesh axis runs over, the one named last changes fastest.
Arguments:
- pool: bfloat16 [16384, 1024], P('shard'), may hold values from -6 to 6
- batch_index: int32 [8192], P('shard'), may hold values from 0 to 1023
- kernel_scale: int32 [1], replicated, may hold values from 4194304 to 8388607
- cotangent: bfloat16 [16, 8192, 1024], P('particle', 'shard'), may hold values from -6 to 6
- weights: float32 [16, 1024, 2, 2048], P('particle', 'shard'), may hold values from -10 to 10
- first_moment: float32 [16, 1024, 2, 2048], P('particle', 'shard'), may hold values from -2 to 2
- second_moment: float32 [16, 1024, 2, 2048], P('particle', 'shard'), may hold values from 0.01 to 1
Outputs:
- new_weights: float32 [16, 1024, 2, 2048], P('particle', 'shard')
- new_first: float32 [16, 1024, 2, 2048], P('particle', 'shard')
- new_second: float32 [16, 1024, 2, 2048], P('particle', 'shard')
- transport: float32 [16, 1024, 2, 2048], P('particle', 'shard')
Inputs may be any that keep to these rules, and one draw needn't show every extreme that they name: `batch_index`: each entry names a row of the pool block that the same index of shard holds.
All inputs are finite; a program needn't handle non-finite values.
Results may differ from a plain program's by a relative error of at most 0.015.
Values may be sent and summed in bfloat16 or wider, within the bound.
A program may use at most 192 MiB of HBM per device.

v0:
```python
import jax
import jax.numpy as jnp
from jax import lax
from jax.sharding import PartitionSpec as P


def gelu_pair(up_proj):
    cdf_part = 0.5 * (1.0 + jax.scipy.special.erf(up_proj * 0.7071067811865476))
    density = jnp.exp(-0.5 * up_proj * up_proj) * 0.3989422804014327
    return (up_proj * cdf_part, cdf_part + up_proj * density)


def local(pool, batch_index, kernel_scale, cotangent, weights, first_moment, second_moment):
    shard_count = lax.axis_size("shard")
    particles = lax.axis_size("particle")
    tok_rows = batch_index.shape[0]
    model_width = pool.shape[1]
    hidden_units = weights.shape[3]
    picked = jnp.take(pool, batch_index, axis=0).astype(jnp.float32)
    normed = (picked * lax.rsqrt(jnp.mean(picked * picked, axis=1, keepdims=True) + 1e-06)).astype(
        jnp.bfloat16
    )
    upstream = cotangent[0]
    local_b = weights[0].astype(jnp.bfloat16)
    block_rows = lax.all_gather(local_b, "shard", axis=0, tiled=True)
    left_cols = normed
    right_cols = upstream
    up_part = jnp.dot(left_cols, block_rows[:, 0, :], preferred_element_type=jnp.float32)
    back_part = jnp.dot(right_cols, block_rows[:, 1, :], preferred_element_type=jnp.float32)
    up_proj = up_part * model_width ** (-0.5)
    back_proj = back_part * hidden_units ** (-0.5)
    act_full, gelu_slope = gelu_pair(up_proj)
    activation = act_full.astype(jnp.bfloat16)
    up_grad = (back_proj * gelu_slope).astype(jnp.bfloat16)
    grad_scale = 1.0 / (tok_rows * shard_count * model_width)
    contract = (((0,), (0,)), ((), ()))
    left_cols = normed
    right_cols = upstream
    g_up = lax.dot_general(left_cols, up_grad, contract, preferred_element_type=jnp.float32)
    g_down = lax.dot_general(right_cols, activation, contract, preferred_element_type=jnp.float32)
    g_up = g_up * (model_width ** (-0.5) * grad_scale)
    g_down = g_down * (hidden_units ** (-0.5) * grad_scale)
    grad_sum = lax.psum_scatter(
        jnp.stack([g_up, g_down], axis=1).astype(jnp.bfloat16),
        "shard",
        scatter_dimension=0,
        tiled=True,
    ).astype(jnp.float32)
    score_b = (-grad_sum).astype(jnp.bfloat16)
    inverse_band = 1.0 / kernel_scale[0].astype(jnp.float32)
    repulse = 2.0 * inverse_band
    own_w = lax.optimization_barrier(local_b).astype(jnp.float32)
    all_w, all_scores = (
        lax.all_gather(local_b[None], "particle", axis=0, tiled=True),
        lax.all_gather(score_b[None], "particle", axis=0, tiled=True),
    )
    all_wf = all_w.astype(jnp.float32)
    offset_sq = own_w[None] - all_wf
    partial_row = jnp.sum(offset_sq * offset_sq, axis=(1, 2, 3))
    distances = lax.psum(partial_row, "shard")
    kernel = jnp.exp(-distances * inverse_band)
    kernel_total = jnp.sum(kernel)
    pushed_field = all_scores.astype(jnp.float32) - repulse * all_wf
    term_rows = (kernel[:, None, None, None] * pushed_field).astype(jnp.bfloat16)
    weighted = jnp.sum(lax.optimization_barrier(term_rows).astype(jnp.float32), axis=0)
    params_total = 2 * model_width * hidden_units
    transport = params_total / particles * (weighted + repulse * kernel_total * own_w)
    new_first = 0.9 * first_moment[0] - 0.1 * transport
    new_second = 0.999 * second_moment[0] + 0.001 * transport * transport
    new_weights = weights[0] - 0.01 * new_first / (jnp.sqrt(new_second) + 1e-08)
    return (new_weights[None], new_first[None], new_second[None], transport[None])


def solution(mesh):
    placed = (
        P("shard", None),
        P("shard"),
        P(),
        P("particle", "shard", None),
        P("particle", "shard", None, None),
        P("particle", "shard", None, None),
        P("particle", "shard", None, None),
    )
    return jax.shard_map(
        local,
        mesh=mesh,
        in_specs=placed,
        out_specs=(
            P("particle", "shard", None, None),
            P("particle", "shard", None, None),
            P("particle", "shard", None, None),
            P("particle", "shard", None, None),
        ),
        check_vma=False,
    )
```

profile of v0, /device:TPU:1, one launch (start us, length us, event | category | flops | bytes accessed | tf_op | source)
XLA Modules:
  0.0 503.9 jit_solution(2273082299362088722)
XLA Ops:
  8.0 0.0 copy-start
  8.0 0.0 all-gather.7.cloned.1.call-start
  8.1 2.6 bitcast_convert_fusion
  10.6 0.0 all-gather.7.cloned.1.call-update
  10.6 0.0 reduce-scatter.2.cloned.1.call-start
  10.7 0.7 compare_select_fusion
  11.4 0.0 copy-done
  11.4 0.0 copy-start.7
  11.4 2.1 gather_fusion
  13.5 0.0 copy-done.7
  13.5 0.4 fusion.9
  13.9 137.3 %all-gather.7.cloned.1.call-done = bf16[1024,2,2048]{2,1,0:T(2,128)(2,1)} async-done(((bf16[64,2,2048]{2,1,0:T(2,128)(2,1)}), bf16[1024,2,2048]{2,1,0:T(2,128)(2,1)}) %all-gather.7.cloned.1.call-update) | async-done | bytes 8388624 | tf_op jit(solution)/shard_map/all_gather | solution.py:25
  151.3 17.1 %fusion.27 = (bf16[1024,1,2048]{2,1,0:T(2,128)(2,1)}, bf16[1024,1,2048]{2,1,0:T(2,128)(2,1)S(1)}) fusion(bf16[1024,2,2048]{2,1,0:T(2,128)(2,1)} %all-gather.7.cloned.1.call-done), kind=kLoop, calls=%fused_computation.51 | loop fusion | bytes 16777216 | tf_op jit(solution)/shard_map/slice | solution.py:29
  168.4 0.0 copy-start.8
  168.4 3.1 fusion.5
  171.6 0.0 copy-done.8
  171.6 0.0 copy-start.9
  171.6 4.2 fusion.8
  175.7 0.0 copy-done.9
  175.7 11.7 %fusion.7 = bf16[1024,1,2048]{2,0,1:T(8,128)(2,1)} fusion(f32[512,2048]{1,0:T(8,128)} %copy-done.9, bf16[1024,1,2048]{2,1,0:T(2,128)(2,1)} %get-tuple-element.10, bf16[1,512,1024]{2,1,0:T(8,128)(2,1)S(1)} %copy-done.8, f32[512]{0:T(512)S(1)} %add_rsqrt_fusion, bf16[512,1024]{1,0:T(8,128)(2,1)S(1)} %gather_fusion, pred[512]{0:T(512)(128)(4,1)S(1)} %compare_and_fusion), kind=kOutput, calls=%fused_computation.19 | convolution fusion | flops 4313841664 | bytes 14682624 | tf_op jit(solution)/shard_map/dot_general | solution.py:39
  187.4 7.5 %pad_maximum_fusion = bf16[1024,2,2048]{2,0,1:T(8,128)(2,1)} fusion(bf16[1024,1,2048]{2,0,1:T(8,128)(2,1)} %fusion.8, bf16[1024,1,2048]{2,0,1:T(8,128)(2,1)} %fusion.7), kind=kLoop, calls=%fused_computation.9 | loop fusion | flops 4194304 | bytes 16777216 | tf_op jit(solution)/shard_map/stack | solution.py:44
  194.9 0.0 reduce-scatter.2.cloned.1.call-update
  194.9 0.2 all-gather.5.cloned.1.call-start
  195.1 1.0 copy-done.2
  196.1 1.4 copy.58
  197.5 0.0 all-gather.5.cloned.1.call-update
  197.5 0.0 all-gather.9.cloned.1.call-start
  197.5 221.5 %reduce-scatter.2.cloned.1.call-done = bf16[64,2,2048]{2,0,1:T(8,128)(2,1)} async-done(((bf16[1024,2,2048]{2,0,1:T(8,128)(2,1)}), bf16[64,2,2048]{2,0,1:T(8,128)(2,1)}) %reduce-scatter.2.cloned.1.call-update) | async-done | bytes 524304 | tf_op jit(solution)/shard_map/reduce_scatter | solution.py:43
  419.0 1.9 negate_convert_fusion
  421.0 0.0 all-gather.9.cloned.1.call-update
  421.0 0.0 copy-done.3
  421.0 0.2 copy.28
  421.9 0.0 all-gather.5.cloned.1.call-done
  421.9 5.7 %fusion.1 = f32[16]{0:T(128)S(1)} fusion(bf16[16,64,2,2048]{3,1,2,0:T(8,128)(2,1)} %all-gather.5.cloned.1.call-done, f32[64,2,2048]{2,0,1:T(8,128)S(1)} %copy.28), kind=kLoop, calls=%fused_computation.4 | loop fusion | flops 16777200 | bytes 9437248 | tf_op jit(solution)/shard_map/reduce_sum | solution.py:59
  427.6 31.4 %psum.7 = f32[16]{0:T(128)S(1)} all-reduce(f32[16]{0:T(128)S(1)} %fusion.1), channel_id=1, replica_groups=mesh['particle'=16,'shard'=16] {'shard'}, use_global_device_ids=true, to_apply=%region_1.2 | all-reduce | flops 16 | bytes 128 | tf_op jit(solution)/shard_map/psum | solution.py:60
  459.0 0.6 fusion.26
  460.3 19.6 %all-gather.9.cloned.1.call-done = bf16[1024,2,2048]{2,0,1:T(8,128)(2,1)} async-done(((bf16[64,2,2048]{2,0,1:T(8,128)(2,1)}), bf16[1024,2,2048]{2,0,1:T(8,128)(2,1)}) %all-gather.9.cloned.1.call-update) | async-done | bytes 8388624 | tf_op jit(solution)/shard_map/all_gather | solution.py:55
  479.9 7.9 %fusion.4 = bf16[16,64,2,2048]{3,1,2,0:T(8,128)(2,1)S(1)} fusion(bf16[16,64,2,2048]{3,1,2,0:T(8,128)(2,1)} %all-gather.5.cloned.1.call-done, f32[]{:T(128)S(6)} %mul_shard_map.3, f32[16]{0:T(128)S(1)} %get-tuple-element.9, bf16[16,64,2,2048]{3,1,0,2:T(8,128)(2,1)} %bitcast.51), kind=kLoop, calls=%fused_computation.7 | loop fusion | flops 25165824 | bytes 25165892 | tf_op jit(solution)/shard_map/convert_element_type | solution.py:64
  487.7 0.0 copy-start.4
  487.7 0.0 copy-start.5
  487.8 0.0 copy-start.6
  487.8 0.0 copy-start.1
  487.8 1.9 convert_reduce_fusion
  489.7 0.0 copy-done.4
  489.7 0.0 copy-done.5
  489.7 0.0 copy-done.6
  489.7 6.8 %fusion.25 = (f32[1,64,2,2048]{3,2,1,0:T(2,128)}, f32[1,64,2,2048]{3,2,1,0:T(2,128)}, f32[1,64,2,2048]{3,2,1,0:T(2,128)}, f32[1,64,2,2048]{3,2,1,0:T(2,128)}) fusion(f32[1,64,2,2048]{3,2,1,0:T(2,128)S(1)} %copy-done.5, bf16[64,2,2048]{2,1,0:T(2,128)(2,1)S(1)} %copy-done.4, f32[]{:T(128)S(6)} %mul.182, f32[64,2,2048]{2,0,1:T(8,128)S(1)} %convert_reduce_fusion, ...), kind=kLoop, calls=%fused_computation.49 | loop fusion | flops 3932160 | bytes 8912900 | tf_op jit(solution)/shard_map/broadcast_in_dim | solution.py:71
  496.5 0.0 copy-done.1
  (5 shorter events, 0.0 us)
Async XLA Ops:
  8.0 3.4 copy-start
  8.0 143.3 %all-gather.7.cloned.1.call-start = ((), (), s32[]{:S(2)}) async-start(), calls=%async_computation.2 | async-start | bytes 8912896 | tf_op jit(solution)/shard_map/all_gather | solution.py:25
  10.6 408.4 %reduce-scatter.2.cloned.1.call-start = ((), (), s32[]{:S(2)}) async-start(), calls=%async_computation.3 | async-start | bytes 8912896 | tf_op jit(solution)/shard_map/reduce_scatter | solution.py:43
  11.4 2.1 copy-start.7
  168.4 3.1 copy-start.8
  171.6 4.2 copy-start.9
  194.9 1.2 copy-start.2
  194.9 226.1 %copy-start.3 = (bf16[64,2,2048]{2,1,0:T(2,128)(2,1)S(1)}, bf16[64,2,2048]{2,1,0:T(2,128)(2,1)}, u32[]{:S(2)}) copy-start(bf16[64,2,2048]{2,1,0:T(2,128)(2,1)} %bitcast_convert_fusion) | copy-start | bytes 1572868
  194.9 227.0 %all-gather.5.cloned.1.call-start = ((), (), s32[]{:S(2)}) async-start(), calls=%async_computation.1 | async-start | bytes 8912896 | tf_op jit(solution)/shard_map/all_gather | solution.py:54
  197.5 282.4 %all-gather.9.cloned.1.call-start = ((), (), s32[]{:S(2)}) async-start(), calls=%async_computation.4 | async-start | bytes 8912896 | tf_op jit(solution)/shard_map/all_gather | solution.py:55
  487.7 1.9 copy-start.4
  487.7 1.9 copy-start.5
  487.8 1.9 copy-start.6
  487.8 8.7 %copy-start.1 = (bf16[1024,1024]{1,0:T(8,128)(2,1)S(1)}, bf16[1024,1024]{1,0:T(8,128)(2,1)}, u32[]{:S(2)}) copy-start(bf16[1024,1024]{1,0:T(8,128)(2,1)} %param.7) | copy-start | bytes 6291460
Sparse Core Ops, SparseCore 0:
  12.0 139.2 all-gather.6
  195.0 223.9 reduce-scatter.1
Sparse Core Ops, SparseCore 1:
  197.8 60.7 all-gather.4
  421.1 58.7 all-gather.8
where the time goes:
time: 504 us
  waiting for transfers between devices  379 us (75%)
  other arithmetic  36 us (7%)
  blocking collectives  31.4 us (6%)
  local copies, waits for them, and re-layouts  21.8 us (4%)
  matrix products  18.9 us (4%)
  between operations  17 us (3%)
    reduce_scatter x1, waiting for transfers between devices, local(): lax.psum_scatter(jnp.stack([g_up, g_down], axis=1).astype(jnp.bfloat16),...  221 us
    all_gather x1, waiting for transfers between devices, local(): block_rows = lax.all_gather(local_b, 'shard', axis=0, tiled=True)  137 us
    psum x1, blocking collectives, local(): distances = lax.psum(partial_row, 'shard')  31.4 us
    all_gather x1, waiting for transfers between devices, local(): lax.all_gather(score_b[None], 'particle', axis=0, tiled=True)  19.6 us
    slice x1, local copies, waits for them, and re-layouts, local(): block_rows[:, 1, :]  17.1 us
    dot_general x1, matrix products, local(): lax.dot_general(left_cols, up_grad, contract, preferred_element_type=jnp....  11.7 us
  transfers between devices with their start and end apart: 4, of which 3 were waited for; matrix products, arithmetic and copies ran while one was open for 3% of the time, Pallas kernels for 0%

commit v1 on v0

--- a/solution.py
+++ b/solution.py
@@ -22,7 +22,15 @@
     )
     upstream = cotangent[0]
     local_b = weights[0].astype(jnp.bfloat16)
-    block_rows = lax.all_gather(local_b, "shard", axis=0, tiled=True)
+    block_rows = jnp.concatenate(
+        lax.all_to_all(
+            jnp.stack(lax.axis_size("shard") * [local_b]),
+            axis_name="shard",
+            split_axis=0,
+            concat_axis=0,
+        ),
+        axis=0,
+    )
     left_cols = normed
     right_cols = upstream
     up_part = jnp.dot(left_cols, block_rows[:, 0, :], preferred_element_type=jnp.float32)

time: 504 us -> 570 us (1.13)
  waiting for transfers between devices: 379 us -> 436 us
  starting transfers between devices: 0.35 us -> 12.2 us
  other arithmetic: 36 us -> 27 us
    all_to_all x0 -> x1, waiting for transfers between devices: none -> 190 us  [local(): lax.all_to_all(jnp.stack(lax.axis_size('shard') * [local_b]), axis_name='...]
    all_gather x1 -> x0, waiting for transfers between devices: 137 us -> none  [local(): block_rows = lax.all_gather(local_b, 'shard', axis=0, tiled=True)]
    slice x1 -> x0, local copies, waits for them, and re-layouts: 17.1 us -> none  [local(): block_rows[:, 1, :]]
    all_to_all x0 -> x1, starting transfers between devices: none -> 11.9 us  [local(): lax.all_to_all(jnp.stack(lax.axis_size('shard') * [local_b]), axis_name='...]
    all_to_all x0 -> x1, local copies, waits for them, and re-layouts: none -> 8.27 us  [local(): lax.all_to_all(jnp.stack(lax.axis_size('shard') * [local_b]), axis_name='...]
    unnamed x21 -> x25, local copies, waits for them, and re-layouts: 2.38 us -> 9.11 us
  transfers between devices with their start and end apart: 4 -> 4, of which waited for: 3 -> 3; matrix products, arithmetic and copies ran while one was open for 3% -> 2% of each run, Pallas kernels for 0% -> 0%
where the time goes in v1:
time: 570 us
  waiting for transfers between devices  436 us (76%)
  blocking collectives  31.2 us (5%)
  other arithmetic  27 us (5%)
  local copies, waits for them, and re-layouts  23.8 us (4%)
  matrix products  21.9 us (4%)
  between operations  17 us (3%)
  starting transfers between devices  12.2 us (2%)
    reduce_scatter x1, waiting for transfers between devices, local(): lax.psum_scatter(jnp.stack([g_up, g_down], axis=1).astype(jnp.bfloat16),...  226 us
    all_to_all x1, waiting for transfers between devices, local(): lax.all_to_all(jnp.stack(lax.axis_size('shard') * [local_b]), axis_name='...  190 us
    psum x1, blocking collectives, local(): distances = lax.psum(partial_row, 'shard')  31.2 us
    all_gather x1, waiting for transfers between devices, local(): lax.all_gather(score_b[None], 'particle', axis=0, tiled=True)  19.7 us
    all_to_all x1, starting transfers between devices, local(): lax.all_to_all(jnp.stack(lax.axis_size('shard') * [local_b]), axis_name='...  11.9 us
  transfers between devices with their start and end apart: 4, of which 3 were waited for; matrix products, arithmetic and copies ran while one was open for 2% of the time, Pallas kernels for 0%

profile of v1, /device:TPU:1, one launch (start us, length us, event | category | flops | bytes accessed | tf_op | source)
XLA Modules:
  0.0 569.5 jit_solution(3399845852195042042)
XLA Ops:
  8.0 0.0 copy-start
  8.0 1.9 copy.53
  10.0 0.0 copy-start.2
  10.0 4.3 stack.11
  14.3 0.0 copy-done.2
  14.3 11.9 %all-to-all-start = ((bf16[16,64,2,2048]{3,1,2,0:T(8,128)(2,1)}), bf16[16,64,2,2048]{3,1,2,0:T(8,128)(2,1)}, u32[]{:S(2)}, u32[]{:S(2)}) async-start(bf16[16,64,2,2048]{3,1,2,0:T(8,128)(2,1)} %stack.11), calls=%async_computation | async-start | bytes 16777216 | tf_op jit(solution)/shard_map/all_to_all | solution.py:26
  26.2 0.0 reduce-scatter.2.cloned.1.call-start
  26.3 0.0 copy-done.8
  26.3 0.0 copy-done
  26.3 2.1 gather_fusion
  28.4 0.4 fusion.9
  28.9 190.2 %all-to-all-done = bf16[16,64,2,2048]{3,1,2,0:T(8,128)(2,1)} async-done(((bf16[16,64,2,2048]{3,1,2,0:T(8,128)(2,1)}), bf16[16,64,2,2048]{3,1,2,0:T(8,128)(2,1)}, u32[]{:S(2)}, u32[]{:S(2)}) %all-to-all-start) | async-done | bytes 8388640 | tf_op jit(solution)/shard_map/all_to_all | solution.py:26
  219.1 8.3 %copy.24 = bf16[16,64,2,2048]{3,1,0,2:T(8,128)(2,1)} copy(bf16[16,64,2,2048]{3,1,2,0:T(8,128)(2,1)} %all-to-all-done) | data formatting | bytes 16777216 | tf_op jit(solution)/shard_map/all_to_all | solution.py:26
  227.4 6.7 %fusion.5 = f32[512,2048]{1,0:T(8,128)} fusion(bf16[1024,2,2048]{2,0,1:T(8,128)(2,1)} %bitcast.58, f32[512]{0:T(512)S(1)} %add_rsqrt_fusion, bf16[512,1024]{1,0:T(8,128)(2,1)S(1)} %gather_fusion, pred[512]{0:T(512)(128)(4,1)S(1)} %compare_and_fusion), kind=kOutput, calls=%fused_computation.13 | convolution fusion | flops 2149580800 | bytes 9439744 | tf_op jit(solution)/shard_map/dot_general | solution.py:36
  234.1 0.0 copy-done.9
  234.1 9.3 %fusion.7 = bf16[1024,1,2048]{2,0,1:T(8,128)(2,1)} fusion(f32[512,2048]{1,0:T(8,128)} %fusion.5, bf16[1024,2,2048]{2,0,1:T(8,128)(2,1)} %bitcast.59, bf16[1,512,1024]{2,1,0:T(8,128)(2,1)S(1)} %copy-done.9, f32[512]{0:T(512)S(1)} %add_rsqrt_fusion, bf16[512,1024]{1,0:T(8,128)(2,1)S(1)} %gather_fusion, pred[512]{0:T(512)(128)(4,1)S(1)} %compare_and_fusion), kind=kOutput, calls=%fused_computation.19 | convolution fusion | flops 4313841664 | bytes 14682624 | tf_op jit(solution)/shard_map/dot_general | solution.py:47
  243.4 5.9 %fusion.8 = bf16[1024,1,2048]{2,0,1:T(8,128)(2,1)} fusion(f32[512,2048]{1,0:T(8,128)} %fusion.5, bf16[1,512,1024]{2,1,0:T(8,128)(2,1)S(1)} %copy-done.9), kind=kOutput, calls=%fused_computation.20 | convolution fusion | flops 2157969408 | bytes 9437184 | tf_op jit(solution)/shard_map/dot_general | solution.py:48
  249.3 0.0 copy-done.5
  249.3 6.2 %pad_maximum_fusion = bf16[1024,2,2048]{2,0,1:T(8,128)(2,1)} fusion(bf16[1024,1,2048]{2,0,1:T(8,128)(2,1)} %fusion.8, bf16[1024,1,2048]{2,0,1:T(8,128)(2,1)S(1)} %copy-done.5), kind=kLoop, calls=%fused_computation.9 | loop fusion | flops 4194304 | bytes 16777216 | tf_op jit(solution)/shard_map/stack | solution.py:52
  255.4 0.0 reduce-scatter.2.cloned.1.call-update
  255.5 0.0 all-gather.4.cloned.1.call-start
  255.5 0.5 all-gather.4.cloned.1.call-update
  256.0 0.2 all-gather.6.cloned.1.call-start
  256.3 225.9 %reduce-scatter.2.cloned.1.call-done = bf16[64,2,2048]{2,0,1:T(8,128)(2,1)} async-done(((bf16[1024,2,2048]{2,0,1:T(8,128)(2,1)}), bf16[64,2,2048]{2,0,1:T(8,128)(2,1)}) %reduce-scatter.2.cloned.1.call-update) | async-done | bytes 524304 | tf_op jit(solution)/shard_map/reduce_scatter | solution.py:51
  482.2 1.9 negate_convert_fusion
  484.1 0.0 all-gather.6.cloned.1.call-update
  484.1 0.0 copy-done.3
  484.1 0.1 convert_element_type.45
  484.9 0.0 all-gather.4.cloned.1.call-done
  485.0 5.7 %fusion.1 = f32[16]{0:T(128)S(1)} fusion(bf16[16,64,2,2048]{3,1,2,0:T(8,128)(2,1)} %all-gather.4.cloned.1.call-done, f32[64,2,2048]{2,0,1:T(8,128)S(1)} %convert_element_type.45), kind=kLoop, calls=%fused_computation.4 | loop fusion | flops 16777200 | bytes 9437248 | tf_op jit(solution)/shard_map/reduce_sum | solution.py:67
  490.7 31.2 %psum.7 = f32[16]{0:T(128)S(1)} all-reduce(f32[16]{0:T(128)S(1)} %fusion.1), channel_id=1, replica_groups=mesh['particle'=16,'shard'=16] {'shard'}, use_global_device_ids=true, to_apply=%region_1.2 | all-reduce | flops 16 | bytes 128 | tf_op jit(solution)/shard_map/psum | solution.py:68
  521.9 0.6 fusion.26
  523.2 19.7 %all-gather.6.cloned.1.call-done = bf16[1024,2,2048]{2,0,1:T(8,128)(2,1)} async-done(((bf16[64,2,2048]{2,0,1:T(8,128)(2,1)}), bf16[1024,2,2048]{2,0,1:T(8,128)(2,1)}) %all-gather.6.cloned.1.call-update) | async-done | bytes 8388624 | tf_op jit(solution)/shard_map/all_gather | solution.py:63
  542.9 7.9 %fusion.4 = bf16[16,64,2,2048]{3,1,2,0:T(8,128)(2,1)S(1)} fusion(bf16[16,64,2,2048]{3,1,2,0:T(8,128)(2,1)} %all-gather.4.cloned.1.call-done, f32[]{:T(128)S(6)} %mul_shard_map.3, f32[16]{0:T(128)S(1)} %get-tuple-element.9, bf16[16,64,2,2048]{3,1,0,2:T(8,128)(2,1)} %bitcast.57), kind=kLoop, calls=%fused_computation.7 | loop fusion | flops 25165824 | bytes 25165892 | tf_op jit(solution)/shard_map/convert_element_type | solution.py:72
  550.8 0.0 copy-start.4
  550.8 0.0 copy-start.6
  550.8 0.0 copy-start.7
  550.8 1.9 convert_reduce_fusion
  552.7 0.0 copy-done.4
  552.7 0.0 copy-done.6
  552.7 0.0 copy-done.7
  552.7 2.2 fusion.18
  555.0 0.0 copy-start.1
  555.0 1.8 copy.28
  556.8 1.8 copy.29
  558.5 1.8 copy.30
  560.3 1.8 copy.31
  562.1 0.0 copy-done.1
  (8 shorter events, 0.0 us)
Async XLA Ops:
  8.0 18.3 %copy-start = (bf16[1024,1024]{1,0:T(8,128)(2,1)S(1)}, bf16[1024,1024]{1,0:T(8,128)(2,1)}, u32[]{:S(2)}) copy-start(bf16[1024,1024]{1,0:T(8,128)(2,1)} %param.7) | copy-start | bytes 6291460
  10.0 4.3 copy-start.2
  14.3 12.0 %copy-start.8 = (s32[512]{0:T(512)S(1)}, s32[512]{0:T(512)}, u32[]{:S(2)}) copy-start(s32[512]{0:T(512)} %param.8) | copy-start | bytes 6148
  14.3 204.8 %all-to-all-start = ((bf16[16,64,2,2048]{3,1,2,0:T(8,128)(2,1)}), bf16[16,64,2,2048]{3,1,2,0:T(8,128)(2,1)}, u32[]{:S(2)}, u32[]{:S(2)}) async-start(bf16[16,64,2,2048]{3,1,2,0:T(8,128)(2,1)} %stack.11), calls=%async_computation | async-start | bytes 16777216 | tf_op jit(solution)/shard_map/all_to_all | solution.py:26
  26.2 455.9 %reduce-scatter.2.cloned.1.call-start = ((), (), s32[]{:S(2)}) async-start(), calls=%async_computation.3 | async-start | bytes 8912896 | tf_op jit(solution)/shard_map/reduce_scatter | solution.py:51
  227.4 6.7 %copy-start.9 = (bf16[1,512,1024]{2,1,0:T(8,128)(2,1)S(1)}, bf16[1,512,1024]{2,1,0:T(8,128)(2,1)}, u32[]{:S(2)}) copy-start(bf16[1,512,1024]{2,1,0:T(8,128)(2,1)} %param.10) | copy-start | bytes 3145732
  243.4 5.9 %copy-start.5 = (bf16[1024,1,2048]{2,0,1:T(8,128)(2,1)S(1)}, bf16[1024,1,2048]{2,0,1:T(8,128)(2,1)}, u32[]{:S(2)}) copy-start(bf16[1024,1,2048]{2,0,1:T(8,128)(2,1)} %fusion.7) | copy-start | bytes 12582916
  255.4 228.7 %copy-start.3 = (bf16[1,64,2,2048]{3,1,2,0:T(8,128)(2,1)S(1)}, bf16[1,64,2,2048]{3,1,2,0:T(8,128)(2,1)}, u32[]{:S(2)}) copy-start(bf16[1,64,2,2048]{3,1,2,0:T(8,128)(2,1)} %copy-done.2) | copy-start | bytes 1572868
  255.5 229.5 %all-gather.4.cloned.1.call-start = ((), (), s32[]{:S(2)}) async-start(), calls=%async_computation.2 | async-start | bytes 8912896 | tf_op jit(solution)/shard_map/all_gather | solution.py:62
  256.0 286.9 %all-gather.6.cloned.1.call-start = ((), (), s32[]{:S(2)}) async-start(), calls=%async_computation.4 | async-start | bytes 8912896 | tf_op jit(solution)/shard_map/all_gather | solution.py:63
  550.8 1.9 copy-start.4
  550.8 1.9 copy-start.6
  550.8 1.9 copy-start.7
  555.0 7.1 %copy-start.1 = (bf16[1024,1024]{1,0:T(8,128)(2,1)S(1)}, bf16[1024,1024]{1,0:T(8,128)(2,1)}, u32[]{:S(2)}) copy-start(bf16[1024,1024]{1,0:T(8,128)(2,1)} %param.7) | copy-start | bytes 6291460
Sparse Core Ops, SparseCore 0:
  255.6 226.5 reduce-scatter.1
Sparse Core Ops, SparseCore 1:
  258.4 63.2 all-gather.3
  484.2 58.6 all-gather.5
